TPU v7x, 256 devices: a whole 4x4x8 slice. The times are simulated.
256 devices in a mesh: dp: 64 (over z, x, y_hi), tok: 4 (over y_lo, core).
Axes of the slice: x: 4, y: 4 (y_hi: 2, y_lo: 2; y = y_hi * 2 + y_lo), z: 8, core: 2. Of those that a mesh axis runs over, the one named last changes fastest.
Arguments:
- acts: bfloat16 [128, 512, 14336], P('dp', 'tok'), may hold values from -30 to 30
- grads: bfloat16 [128, 512, 4096], P('dp', 'tok'), may hold values from -30 to 30
- lengths: int32 [128], P('dp'), may hold values from 1 to 512, as said below
- domains: int32 [128, 1], replicated, may hold values from 0 to 15
- hash_salts: int32 [2], replicated, may hold values from 0 to 46336
Outputs:
- example_grads: bfloat16 [128, 65536], P('dp', 'tok')
- kernel: float32 [16, 16], replicated
Inputs may be any that keep to these rules, and one draw needn't show every extreme that they name: `lengths`: some example has all 512 slots live in every draw. `domains`: every domain holds at least one example.
All inputs are finite; a program needn't handle non-finite values.
Results may differ from a plain program's by a relative error of at most 0.0057.
Values may be sent and summed in bfloat16 or wider, within the bound.
A program may use at most 128 MiB of HBM per device.

v0:
```python
import math

import jax
import jax.numpy as jnp
from jax import lax
from jax.sharding import PartitionSpec as P

KX = 256
KG = 256
LEN = 512
DOMAINS = 16


def sign_table(rows, cols, salt_value):
    row_idx = lax.broadcasted_iota(jnp.int32, (rows, cols), 0)
    col_idx = lax.broadcasted_iota(jnp.int32, (rows, cols), 1)
    first = (row_idx * 7919 + col_idx * 6007 + salt_value) % 46337
    second = (first * first + 3 * row_idx + col_idx) % 46337
    third = (second * second + salt_value) % 46337
    return jnp.where(third % 2 == 1, 1.0, -1.0).astype(jnp.bfloat16)


def domain_rows(labels, count):
    columns = lax.broadcasted_iota(jnp.int32, (labels.shape[0], count), 1)
    return (labels[:, None] == columns).astype(jnp.float32)


def body(acts, grads, lengths, domains, hash_salts):
    ex_dev, seg, width_x = acts.shape
    width_g = grads.shape[2]
    table_x = sign_table(width_x, KX, hash_salts[0])
    table_g = sign_table(width_g, KG, hash_salts[1])
    position = lax.axis_index("tok") * seg + lax.broadcasted_iota(jnp.int32, (ex_dev, seg), 1)
    live = (position < lengths[:, None]).astype(jnp.float32)[:, :, None]
    proj_x = (
        jnp.einsum("etf,fk->etk", acts, table_x, preferred_element_type=jnp.float32)
        * (live / math.sqrt(width_x))
    ).astype(jnp.bfloat16)
    proj_g = (
        jnp.einsum("etf,fk->etk", grads, table_g, preferred_element_type=jnp.float32)
        * (live / math.sqrt(width_g))
    ).astype(jnp.bfloat16)
    partial_value = jnp.einsum(
        "etg,etk->egk", proj_g, proj_x, preferred_element_type=jnp.float32
    ).reshape(ex_dev, KG * KX)
    summed = lax.psum_scatter(partial_value, "tok", scatter_dimension=1, tiled=True)
    example_grads = (summed / math.sqrt(LEN)).astype(jnp.bfloat16)
    all_hot = domain_rows(domains[:, 0], DOMAINS)
    here = lax.axis_index("dp")
    own_hot = lax.dynamic_slice_in_dim(all_hot, here * ex_dev, ex_dev, 0)
    local_sums = jnp.dot(
        own_hot.T, example_grads.astype(jnp.float32), precision=lax.Precision.HIGHEST
    )
    share = lax.psum_scatter(local_sums, "dp", scatter_dimension=1, tiled=True)
    gram_part = jnp.dot(share, share.T, precision=lax.Precision.HIGHEST)
    kernel_sum = lax.psum(gram_part, ("dp", "tok"))
    kernel = kernel_sum / (16.0 * KX * KG)
    return (example_grads, kernel)


def solution(mesh):
    in_specs = (P("dp", "tok", None), P("dp", "tok", None), P("dp"), P(), P())
    out_specs = (P("dp", "tok"), P())
    return jax.shard_map(body, mesh=mesh, in_specs=in_specs, out_specs=out_specs, check_vma=False)
```

profile of v0, /device:TPU:1, one launch (start us, length us, event | category | flops | bytes accessed | tf_op | source)
XLA Modules:
  0.0 815.2 jit_solution(1765495702421940392)
XLA Ops:
  7.2 0.0 copy-start
  7.2 0.0 reduce-scatter.7.cloned.1.call-start
  7.3 1.4 fusion.94
  8.7 0.7 compare_select_fusion
  9.4 0.0 copy-done
  9.4 0.0 copy-start.2
  9.4 11.3 %fusion.68 = bf16[2,128,256]{1,2,0:T(8,128)(2,1)S(1)} fusion(bf16[2,128,4096]{2,1,0:T(8,128)(2,1)S(1)} %copy-done, s32[4096]{0:T(1024)S(1)} %get-tuple-element.6, s32[]{:T(128)} %bitcast, s32[256]{0:T(256)S(1)} %iota_multiply_fusion.4, s32[4096]{0:T(1024)S(1)} %get-tuple-element.7, f32[2,128]{1,0:T(2,128)S(1)} %get-tuple-element.3), kind=kOutput, calls=%fused_computation.70 | convolution fusion | flops 577896448 | bytes 2263044 | tf_op jit(solution)/shard_map/etf,fk->etk/dot_general | solution.py:40
  20.8 0.0 copy-done.2
  20.8 38.4 %fusion.62.clone.4 = bf16[2,128,256]{2,1,0:T(8,128)(2,1)S(1)} fusion(bf16[2,128,14336]{2,1,0:T(8,128)(2,1)S(1)} %copy-done.2, s32[14336]{0:T(1024)S(1)} %get-tuple-element.8, s32[]{:T(128)} %bitcast.3, s32[256]{0:T(256)S(1)} %iota_multiply_fusion.4, s32[14336]{0:T(1024)S(1)} %get-tuple-element.9, f32[2,128]{1,0:T(2,128)S(1)} %get-tuple-element.2), kind=kOutput, calls=%fused_computation.68.clone.clone.clone.1 | convolution fusion | flops 2022309888 | bytes 7587844 | tf_op jit(solution)/shard_map/etf,fk->etk/dot_general | solution.py:36
  59.1 0.2 fusion.66
  59.3 16.4 %copy.9 = f32[2,256,256]{0,2,1:T(8,128)} copy(f32[2,256,256]{2,1,0:T(8,128)S(1)} %fusion.66) | data formatting | bytes 1048576
  75.7 0.0 copy-start.3
  75.7 0.0 reduce-scatter.7.cloned.1.call-update
  75.8 0.0 reduce-scatter.5.cloned.1.call-start
  75.8 0.6 copy-done.3
  76.4 0.1 dynamic-slice
  76.5 287.4 %reduce-scatter.7.cloned.1.call-done = f32[16384,2]{1,0:T(8,128)} async-done(((f32[65536,2]{1,0:T(8,128)}), f32[16384,2]{1,0:T(8,128)}) %reduce-scatter.7.cloned.1.call-update) | async-done | bytes 131088
  363.8 5.3 copy.8
  369.2 0.1 multiply_convert_fusion
  369.2 0.0 copy-start.1
  369.3 1.4 fusion.72
  370.7 0.0 reduce-scatter.5.cloned.1.call-update
  370.7 311.9 %reduce-scatter.5.cloned.1.call-done = f32[16,256]{1,0:T(8,128)} async-done(((f32[16,16384]{1,0:T(8,128)}), f32[16,256]{1,0:T(8,128)}) %reduce-scatter.5.cloned.1.call-update) | async-done | bytes 16400 | tf_op jit(solution)/shard_map/reduce_scatter | solution.py:54
  682.6 0.9 fusion.95
  683.5 124.2 %psum.7 = f32[16,16]{1,0:T(8,128)S(1)} all-reduce(f32[16,16]{1,0:T(8,128)S(1)} %fusion.95), channel_id=1, replica_groups=mesh['dp'=64,'tok'=4] {'dp','tok'}, use_global_device_ids=true, to_apply=%region_2.3 | all-reduce | flops 256 | bytes 2048 | tf_op jit(solution)/shard_map/psum | solution.py:56
  807.7 0.6 broadcast_multiply_fusion
  808.3 0.0 copy-done.1
  (4 shorter events, 0.0 us)
Async XLA Ops:
  7.2 2.2 copy-start
  7.2 356.6 %reduce-scatter.7.cloned.1.call-start = ((), (), s32[]{:S(2)}) async-start(), calls=%async_computation.3 | async-start | bytes 41943040
  9.4 11.4 %copy-start.2 = (bf16[2,128,14336]{2,1,0:T(8,128)(2,1)S(1)}, bf16[2,128,14336]{2,1,0:T(8,128)(2,1)}, u32[]{:S(2)}) copy-start(bf16[2,128,14336]{2,1,0:T(8,128)(2,1)} %param.5) | copy-start | bytes 22020100
  75.7 0.7 copy-start.3
  75.8 606.8 %reduce-scatter.5.cloned.1.call-start = ((), (), s32[]{:S(2)}) async-start(), calls=%async_computation.2 | async-start | bytes 1064960 | tf_op jit(solution)/shard_map/reduce_scatter | solution.py:54
  369.2 439.1 %copy-start.1 = (bf16[2,16384]{1,0:T(2,128)(2,1)}, bf16[2,16384]{1,0:T(2,128)(2,1)S(1)}, u32[]{:S(2)}) copy-start(bf16[2,16384]{1,0:T(2,128)(2,1)S(1)} %multiply_convert_fusion) | copy-start | bytes 196612
Sparse Core Ops, SparseCore 0:
  75.9 287.8 reduce-scatter.6
  370.8 311.6 reduce-scatter.4
where the time goes:
time: 816 us; the launch traced here: 815 us
  waiting for transfers between devices  599 us (73%)
  blocking collectives  124 us (15%)
  matrix products  52.3 us (6%)
  local copies, waits for them, and re-layouts  23.8 us (3%)
  between operations  14.1 us (2%)
    reduce_scatter x1, waiting for transfers between devices, body(): share = lax.psum_scatter(local_sums, 'dp', scatter_dimension=1, tiled=True)  312 us
    unnamed x3, waiting for transfers between devices  287 us
    psum x1, blocking collectives, body(): kernel_sum = lax.psum(gram_part, ('dp', 'tok'))  124 us
    dot_general x1, matrix products, body(): jnp.einsum('etf,fk->etk', acts, table_x, preferred_element_type=jnp.float32)  38.4 us
    unnamed x10, local copies, waits for them, and re-layouts  22.3 us
  transfers between devices with their start and end apart: 2, of which 2 were waited for; matrix products, arithmetic and copies ran while one was open for 0% of the time, Pallas kernels for 0%

commit v1 on v0

v1 whole, which is shorter than its diff:
```python
import functools
import math

import jax
import jax.numpy as jnp
import numpy as np
from jax import lax
from jax.experimental import pallas as pl
from jax.experimental.pallas import tpu as pltpu
from jax.sharding import PartitionSpec as P

KX = 256
KG = 256
LEN = 512
DOMAINS = 16
MESH = pl.DeviceIdType.MESH

PR = 46337
INV2 = (PR + 1) // 2
HALF_ROOT = 19963
UNIT = HALF_ROOT * pow(2, 16, PR) % PR
BACK = pow(pow(2, 32, PR), -1, PR)
TURN = (BACK * 2**32 - 1) // PR
STEP_WHOLE = 2**32 // PR
STEP_REST = 2**32 % PR
BIAS = 46343
ROWS = 1024
PAIR = 2 * ROWS


def centered(value):
    value = value % PR
    return value - PR if value > PR // 2 else value


def row_matrix(chunks):
    local = np.arange(ROWS)
    b, a, z = local // 128, local // 8 % 16, local % 8
    out = np.zeros((ROWS, 128), np.float32)
    for offset, digit in ((0, b), (8, b), (16, a), (32, a), (48, z), (56, z)):
        out[local, offset + digit] = 1.0
    for g in range(chunks):
        cross = (ROWS * g + 128 * b) * (8 * a + z) + 8 * a * z
        value = (2 * UNIT * 7919 * 7919 % PR) * (cross % PR) % PR
        value = np.where(value > PR // 2, value - PR, value)
        high = np.round(value / 256)
        out[:, 64 + 2 * g] = high
        out[:, 65 + 2 * g] = value - 256 * high
    return out


def reduced(value):
    return value - float(PR) * jnp.round(value * (1.0 / PR))


def digits(value):
    high = jnp.round(value * (1.0 / 256))
    return high, value - 256.0 * high


def product(left, right):
    high, low = digits(left)
    return reduced(high * reduced(256.0 * right) + low * right)


def iotas(rows):
    row = lax.broadcasted_iota(jnp.int32, (rows, KX), 0).astype(jnp.float32)
    col = lax.broadcasted_iota(jnp.int32, (rows, KX), 1).astype(jnp.float32)
    return row, col


def linear_terms(rows, unit, beta):
    row, _ = iotas(rows)
    slope = reduced(float(centered(2 * UNIT * 7919 * unit)) * row)
    square = reduced(float(centered(UNIT * 7919 * 7919 * unit * unit)) * (row * row))
    line = reduced(float(centered(3 * UNIT * unit)) * row)
    return reduced(product(slope, beta) + square + line)


def column_tables(salt, chunks, first, rall):
    salt = salt.astype(jnp.float32)

    def beta(rows):
        _, col = iotas(rows)
        return reduced(6007.0 * col + salt)

    row, col = iotas(8 * chunks)
    inner = reduced(reduced(float(centered(7919 * 128)) * row) + beta(8 * chunks))
    value = reduced(product(inner, inner) + (384.0 * row + col))
    base_high, base_low = digits(product(jnp.full_like(value, float(centered(UNIT))), value))
    mid_high, mid_low = digits(linear_terms(16, 8, beta(16)))
    low_high, low_low = digits(linear_terms(8, 1, beta(8)))
    pick = lax.broadcasted_iota(jnp.int32, (64, KX), 0)
    for g in range(chunks):
        cross = jnp.where(pick == 2 * g, 256.0, jnp.where(pick == 2 * g + 1, 1.0, 0.0))
        rall[first + g] = jnp.concatenate(
            [
                256.0 * base_high[8 * g : 8 * g + 8],
                base_low[8 * g : 8 * g + 8],
                256.0 * mid_high,
                mid_low,
                256.0 * low_high,
                low_low,
                cross,
            ],
            axis=0,
        ).astype(jnp.bfloat16)


def salt_turn(salt):
    half = jnp.where(salt % 2 == 1, (salt + PR) // 2, salt // 2)
    whole = half * jnp.int32(STEP_WHOLE - 2**32 if STEP_WHOLE >= 2**31 else STEP_WHOLE)
    return whole + (half * STEP_REST) // PR + BIAS


def kernel(
    width_x,
    width_g,
    lengths_ref,
    salts_ref,
    acts_ref,
    grads_ref,
    rows_ref,
    domains_ref,
    eg_ref,
    out_ref,
    xbuf,
    table,
    rall,
    acc,
    part,
    tok_send,
    tok_slot,
    msg,
    dom_slot,
    sums,
    sum_slot,
    gram_b,
    gram_a,
    in_sem,
    tok_ss,
    tok_rs,
    msg_ss,
    msg_rs,
    sum_ss,
    sum_rs,
    gb_ss,
    gb_rs,
    ga_ss,
    ga_rs,
):
    dp, tok = lax.axis_index("dp"), lax.axis_index("tok")
    z, x, yh = dp // 8, (dp // 2) % 4, dp % 2
    ia, ib = z * 2 + yh, x * 4 + tok

    def peer_a(i):
        return ((i // 2) * 8 + x * 2 + i % 2, tok)

    def peer_b(i):
        return (z * 8 + (i // 4) * 2 + yh, i % 4)

    n_g, n_x = width_g // PAIR, width_x // PAIR
    n = n_g + n_x
    loads = [
        pltpu.make_async_copy(grads_ref.at[:, pl.ds(c * PAIR, PAIR)], xbuf.at[c], in_sem.at[c])
        for c in range(n_g)
    ] + [
        pltpu.make_async_copy(
            acts_ref.at[:, pl.ds(c * PAIR, PAIR)], xbuf.at[n_g + c], in_sem.at[n_g + c]
        )
        for c in range(n_x)
    ]
    for load in loads:
        load.start()

    barrier = pltpu.get_barrier_semaphore()

    def greet(k, _):
        pl.semaphore_signal(barrier, inc=1, device_id=peer_a((ia + k) % 16), device_id_type=MESH)
        pl.semaphore_signal(barrier, inc=1, device_id=peer_b((ib + k) % 16), device_id_type=MESH)
        return 0

    lax.fori_loop(1, 16, greet, 0)

    salt_x, salt_g = salts_ref[0], salts_ref[1]
    column_tables(salt_g, 2 * n_g, 0, rall)
    column_tables(salt_x, 2 * n_x, 2 * n_g, rall)
    turn_x, turn_g = salt_turn(salt_x), salt_turn(salt_g)
    acc[...] = jnp.zeros_like(acc)

    def make_table(c, slot):
        turn = jnp.where(c < n_g, turn_g, turn_x)
        for half in range(2):
            value = jnp.dot(rows_ref[...], rall[2 * c + half], preferred_element_type=jnp.float32)
            small = (jnp.abs(value) - float(PR)).astype(jnp.int32)
            angle = small * small * jnp.int32(TURN - 2**32) + turn
            sign = jnp.where(angle < 0, 1.0, -1.0).astype(jnp.bfloat16)
            table[slot, pl.ds(half * ROWS, ROWS), :] = sign

    def project(c, slot):
        which = jnp.where(c < n_g, 0, 1)
        pltpu.make_async_copy(acts_ref.at[:, pl.ds(0, PAIR)], xbuf.at[c], in_sem.at[c]).wait()
        acc[which] += jnp.dot(xbuf[c], table[slot], preferred_element_type=jnp.float32)

    make_table(0, 0)

    def step(c, _):
        slot = lax.rem(c, 2)
        project(c, slot)
        make_table(c + 1, 1 - slot)
        return 0

    lax.fori_loop(0, n - 1, step, 0)
    project(n - 1, (n - 1) % 2)

    seg = acc.shape[1] // 2
    position = tok * seg + lax.broadcasted_iota(jnp.int32, (seg, KX), 0)
    for e in range(2):
        live = (position < lengths_ref[e]).astype(jnp.float32)
        rows = pl.ds(e * seg, seg)
        proj_g = (acc[0, rows, :] * (live / math.sqrt(width_g))).astype(jnp.bfloat16)
        proj_x = (acc[1, rows, :] * (live / math.sqrt(width_x))).astype(jnp.bfloat16)
        outer = lax.dot_general(
            proj_g, proj_x, (((0,), (0,)), ((), ())), preferred_element_type=jnp.float32
        )
        for q in range(4):
            block = outer[64 * q : 64 * q + 64]
            part[q, e] = block
            tok_send[q, e] = block.astype(jnp.bfloat16)

    pl.semaphore_wait(barrier, 30)

    def tok_copy(k):
        to = (tok + k) % 4
        return pltpu.make_async_remote_copy(
            src_ref=tok_send.at[to],
            dst_ref=tok_slot.at[tok],
            send_sem=tok_ss.at[k],
            recv_sem=tok_rs.at[tok],
            device_id=(dp, to),
            device_id_type=MESH,
        )

    def tok_arrival(k):
        source = (tok + k) % 4
        return pltpu.make_async_remote_copy(
            src_ref=tok_send.at[source],
            dst_ref=tok_slot.at[source],
            send_sem=tok_ss.at[k],
            recv_sem=tok_rs.at[source],
            device_id=(dp, source),
            device_id_type=MESH,
        )

    for k in range(1, 4):
        tok_copy(k).start()

    lane = lax.broadcasted_iota(jnp.int32, (128, 256), 1)
    row = lax.broadcasted_iota(jnp.int32, (128, 256), 0)
    source = lane // 16
    example = 2 * ((source // 2) * 8 + x * 2 + source % 2) + (lane // 8) % 2
    chosen = (row == example).astype(jnp.bfloat16)
    labels = jnp.broadcast_to(domains_ref[...], (8, 128)).astype(jnp.float32).astype(jnp.bfloat16)
    label = jnp.dot(labels, chosen, preferred_element_type=jnp.float32)[0:1].astype(jnp.int32)
    hot = ((label == row % 16) & (row // 16 == lane % 8)).astype(jnp.float32).astype(jnp.bfloat16)

    for k in range(1, 4):
        tok_arrival(k).wait_recv()
    total = part[tok]
    for k in range(1, 4):
        total = total + tok_slot[(tok + k) % 4].astype(jnp.float32)
    total = total / math.sqrt(LEN)
    eg_ref[...] = total.astype(jnp.bfloat16)
    for t in range(16):
        r, c = 8 * (t // 2), 128 * (t % 2)
        msg[t] = jnp.concatenate(
            [total[0, r : r + 8, c : c + 128], total[1, r : r + 8, c : c + 128]], axis=0
        ).astype(jnp.bfloat16)

    def msg_copy(k):
        to = (ia + k) % 16
        return pltpu.make_async_remote_copy(
            src_ref=msg.at[to],
            dst_ref=dom_slot.at[ia],
            send_sem=msg_ss.at[k],
            recv_sem=msg_rs.at[ia],
            device_id=peer_a(to),
            device_id_type=MESH,
        )

    def msg_arrival(k):
        source = (ia + k) % 16
        return pltpu.make_async_remote_copy(
            src_ref=msg.at[source],
            dst_ref=dom_slot.at[source],
            send_sem=msg_ss.at[k],
            recv_sem=msg_rs.at[source],
            device_id=peer_a(source),
            device_id_type=MESH,
        )

    def each(count, action):
        def once(k, _):
            action(k)
            return 0

        lax.fori_loop(1, count, once, 0)

    each(16, lambda k: msg_copy(k).start())
    dom_slot[ia] = msg[ia]
    each(16, lambda k: msg_arrival(k).wait_recv())
    held = dom_slot[...].reshape(256, 128)
    domain_part = jnp.dot(hot, held, preferred_element_type=jnp.float32)
    for q in range(4):
        sums[q] = domain_part[32 * q : 32 * q + 32]

    def sum_copy(k):
        to = (x + k) % 4
        return pltpu.make_async_remote_copy(
            src_ref=sums.at[to],
            dst_ref=sum_slot.at[x],
            send_sem=sum_ss.at[k],
            recv_sem=sum_rs.at[x],
            device_id=(z * 8 + to * 2 + yh, tok),
            device_id_type=MESH,
        )

    def sum_arrival(k):
        source = (x + k) % 4
        return pltpu.make_async_remote_copy(
            src_ref=sums.at[source],
            dst_ref=sum_slot.at[source],
            send_sem=sum_ss.at[k],
            recv_sem=sum_rs.at[source],
            device_id=(z * 8 + source * 2 + yh, tok),
            device_id_type=MESH,
        )

    for k in range(1, 4):
        sum_copy(k).start()
    sum_slot[x] = sums[x]
    for k in range(1, 4):
        sum_arrival(k).wait_recv()
    share = (sum_slot[0] + sum_slot[1]) + (sum_slot[2] + sum_slot[3])
    wide = jnp.zeros((16, 128), jnp.float32)
    for r in range(2):
        own = share[16 * r : 16 * r + 16]
        wide = wide + lax.dot_general(
            own,
            jnp.concatenate([own] * 8, axis=0),
            (((1,), (1,)), ((), ())),
            precision=lax.Precision.HIGHEST,
            preferred_element_type=jnp.float32,
        )
    on_diagonal = (
        lax.broadcasted_iota(jnp.int32, (16, 128), 1) // 16
        == lax.broadcasted_iota(jnp.int32, (16, 128), 0) % 8
    )
    wide = jnp.where(on_diagonal, wide, 0.0)
    flat = jnp.concatenate(
        [jnp.sum(wide[:8], axis=0, keepdims=True), jnp.sum(wide[8:], axis=0, keepdims=True)], axis=0
    )

    def gram_copy(slots, sends, receives, me, peer, k, to):
        return pltpu.make_async_remote_copy(
            src_ref=slots.at[me],
            dst_ref=slots.at[to],
            send_sem=sends.at[k],
            recv_sem=receives.at[to],
            device_id=peer((me + k) % 16),
            device_id_type=MESH,
        )

    for slots, sends, receives, me, peer in (
        (gram_b, gb_ss, gb_rs, ib, peer_b),
        (gram_a, ga_ss, ga_rs, ia, peer_a),
    ):
        slots[me] = flat
        copy = functools.partial(gram_copy, slots, sends, receives, me, peer)
        each(16, lambda k: copy(k, me).start())
        each(16, lambda k: copy(k, (me + k) % 16).wait_recv())
        flat = jnp.sum(slots[...], axis=0)

    spread = jnp.concatenate(
        [jnp.broadcast_to(flat[0:1], (8, 128)), jnp.broadcast_to(flat[1:2], (8, 128))], axis=0
    )
    spread = jnp.where(on_diagonal, spread, 0.0)
    fold = (
        lax.broadcasted_iota(jnp.int32, (128, 16), 0) % 16
        == lax.broadcasted_iota(jnp.int32, (128, 16), 1)
    ).astype(jnp.float32)
    out_ref[...] = jnp.dot(
        spread, fold, precision=lax.Precision.HIGHEST, preferred_element_type=jnp.float32
    ) / (16.0 * KX * KG)

    for k in range(1, 4):
        tok_copy(k).wait_send()
        sum_copy(k).wait_send()
    each(16, lambda k: msg_copy(k).wait_send())
    each(16, lambda k: gram_copy(gram_b, gb_ss, gb_rs, ib, peer_b, k, ib).wait_send())
    each(16, lambda k: gram_copy(gram_a, ga_ss, ga_rs, ia, peer_a, k, ia).wait_send())


def body(acts, grads, lengths, domains, hash_salts):
    ex_dev, seg, width_x = acts.shape
    width_g = grads.shape[2]
    tokens = ex_dev * seg
    chunks = (width_x + width_g) // PAIR
    rows = jnp.asarray(row_matrix(width_x // ROWS), jnp.bfloat16)
    dma = pltpu.SemaphoreType.DMA
    grads_out, gram = pl.pallas_call(
        functools.partial(kernel, width_x, width_g),
        out_shape=(
            jax.ShapeDtypeStruct((ex_dev, 64, KX), jnp.bfloat16),
            jax.ShapeDtypeStruct((DOMAINS, DOMAINS), jnp.float32),
        ),
        in_specs=[
            pl.BlockSpec(memory_space=pltpu.SMEM),
            pl.BlockSpec(memory_space=pltpu.SMEM),
            pl.BlockSpec(memory_space=pl.ANY),
            pl.BlockSpec(memory_space=pl.ANY),
            pl.BlockSpec(memory_space=pltpu.VMEM),
            pl.BlockSpec(memory_space=pltpu.VMEM),
        ],
        out_specs=(
            pl.BlockSpec(memory_space=pltpu.VMEM),
            pl.BlockSpec(memory_space=pltpu.VMEM),
        ),
        scratch_shapes=[
            pltpu.VMEM((chunks, tokens, PAIR), jnp.bfloat16),
            pltpu.VMEM((2, PAIR, KX), jnp.bfloat16),
            pltpu.VMEM((2 * chunks, 128, KX), jnp.bfloat16),
            pltpu.VMEM((2, tokens, KX), jnp.float32),
            pltpu.VMEM((4, 2, 64, KX), jnp.float32),
            pltpu.VMEM((4, 2, 64, KX), jnp.bfloat16),
            pltpu.VMEM((4, 2, 64, KX), jnp.bfloat16),
            pltpu.VMEM((16, 16, 128), jnp.bfloat16),
            pltpu.VMEM((16, 16, 128), jnp.bfloat16),
            pltpu.VMEM((4, 32, 128), jnp.float32),
            pltpu.VMEM((4, 32, 128), jnp.float32),
            pltpu.VMEM((16, 2, 128), jnp.float32),
            pltpu.VMEM((16, 2, 128), jnp.float32),
            dma((chunks,)),
            dma((4,)),
            dma((4,)),
            dma((16,)),
            dma((16,)),
            dma((4,)),
            dma((4,)),
            dma((16,)),
            dma((16,)),
            dma((16,)),
            dma((16,)),
        ],
        compiler_params=pltpu.CompilerParams(
            collective_id=0, has_side_effects=True, vmem_limit_bytes=56 << 20
        ),
    )(
        lengths,
        hash_salts,
        acts.reshape(tokens, width_x),
        grads.reshape(tokens, width_g),
        rows,
        domains.reshape(1, domains.shape[0]),
    )
    return grads_out.reshape(ex_dev, 64 * KX), gram


def solution(mesh):
    in_specs = (P("dp", "tok", None), P("dp", "tok", None), P("dp"), P(), P())
    out_specs = (P("dp", "tok"), P())
    return jax.shard_map(body, mesh=mesh, in_specs=in_specs, out_specs=out_specs, check_vma=False)
```

time: 816 us -> 46.1 us (0.06)
  waiting for transfers between devices: 599 us -> 0 us
  blocking collectives: 124 us -> 0 us
  matrix products: 52.3 us -> 0 us
  Pallas kernels: 0 us -> 42.5 us
  local copies, waits for them, and re-layouts: 23.8 us -> 2.83 us
  between operations: 14.1 us -> 0.64 us
    reduce_scatter x1 -> x0, waiting for transfers between devices: 312 us -> none  [body(): share = lax.psum_scatter(local_sums, 'dp', scatter_dimension=1, tiled=True)]
    unnamed x3 -> x0, waiting for transfers between devices: 287 us -> none
    psum x1 -> x0, blocking collectives: 124 us -> none  [body(): kernel_sum = lax.psum(gram_part, ('dp', 'tok'))]
    dot_general x5 -> x0, matrix products: 52.3 us -> none  [the longest x1 38.4 us: body(): jnp.einsum('etf,fk->etk', acts, table_x, preferred_element_type=jnp.float32)]
    pallas_call x0 -> x1, Pallas kernels: none -> 42.5 us  [body(): pl.pallas_call(functools.partial(kernel, width_x, width_g), out_shape=(ja...]
    unnamed x10 -> x2, local copies, waits for them, and re-layouts: 22.3 us -> 2.83 us
  transfers between devices with their start and end apart: 2 -> 0, of which waited for: 2 -> 0; matrix products, arithmetic and copies ran while one was open for 0% -> 0% of each run, Pallas kernels for 0% -> 0%
where the time goes in v1:
time: 46.1 us; the launch traced here: 45.9 us
  Pallas kernels  42.5 us (92%)
  local copies, waits for them, and re-layouts  2.83 us (6%)
  between operations  0.64 us (1%)
    pallas_call x1, Pallas kernels, body(): pl.pallas_call(functools.partial(kernel, width_x, width_g), out_shape=(ja...  42.5 us
    unnamed x2, local copies, waits for them, and re-layouts  2.83 us

profile of v1, /device:TPU:1, one launch (start us, length us, event | category | flops | bytes accessed | tf_op | source)
XLA Modules:
  0.0 45.9 jit_solution(8365378395227423329)
XLA Ops:
  0.6 42.5 %shard_map.77 = (bf16[2,64,256]{2,1,0:T(8,128)(2,1)}, f32[16,16]{1,0:T(8,128)}) custom-call(s32[2]{0:T(128)} %lengths_ref.1, s32[2]{0:T(128)} %salts_ref.1, bf16[256,14336]{1,0:T(8,128)(2,1)} %bitcast.5, bf16[256,4096]{1,0:T(8,128)(2,1)} %bitcast.6, bf16[1024,128]{1,0:T(8,128)(2,1)} %constant.2.clone.rows_ref, s32[1,128]{1,0:T(1,128)} %bitcast.9), custom_call_target="tpu_custom_call" | custom-call | tf_op jit(solution)/shard_map/pallas_call | solution.py:411
  43.1 1.5 %copy.8 = bf16[1,2,64,256]{3,1,2,0:T(2,128)(2,1)} copy(bf16[1,2,64,256]{3,2,1,0:T(8,128)(2,1)} %bitcast.8) | data formatting | bytes 131072
  44.6 1.3 %copy.10 = f32[16,16]{1,0:T(8,128)} copy(f32[16,16]{1,0:T(8,128)} %get-tuple-element.9) | data formatting | bytes 2048

commit v2 on v1

v2 whole, which is shorter than its diff:
```python
import functools
import math

import jax
import jax.numpy as jnp
import numpy as np
from jax import lax
from jax.experimental import pallas as pl
from jax.experimental.pallas import tpu as pltpu
from jax.sharding import PartitionSpec as P

KX = 256
KG = 256
LEN = 512
DOMAINS = 16
MESH = pl.DeviceIdType.MESH

PR = 46337
INV2 = (PR + 1) // 2
HALF_ROOT = 19963
UNIT = HALF_ROOT * pow(2, 16, PR) % PR
BACK = pow(pow(2, 32, PR), -1, PR)
TURN = (BACK * 2**32 - 1) // PR
STEP_WHOLE = 2**32 // PR
STEP_REST = 2**32 % PR
BIAS = 46343
ROWS = 1024
PAIR = 2 * ROWS


def centered(value):
    value = value % PR
    return value - PR if value > PR // 2 else value


def row_matrix(chunks):
    local = np.arange(ROWS)
    b, a, z = local // 128, local // 8 % 16, local % 8
    out = np.zeros((ROWS, 128), np.float32)
    for offset, digit in ((0, b), (8, b), (16, a), (32, a), (48, z), (56, z)):
        out[local, offset + digit] = 1.0
    for g in range(chunks):
        cross = (ROWS * g + 128 * b) * (8 * a + z) + 8 * a * z
        value = (2 * UNIT * 7919 * 7919 % PR) * (cross % PR) % PR
        value = np.where(value > PR // 2, value - PR, value)
        high = np.round(value / 256)
        out[:, 64 + 2 * g] = high
        out[:, 65 + 2 * g] = value - 256 * high
    return out


def reduced(value):
    return value - float(PR) * jnp.round(value * (1.0 / PR))


def digits(value):
    high = jnp.round(value * (1.0 / 256))
    return high, value - 256.0 * high


def product(left, right):
    high, low = digits(left)
    return reduced(high * reduced(256.0 * right) + low * right)


def iotas(rows):
    row = lax.broadcasted_iota(jnp.int32, (rows, KX), 0).astype(jnp.float32)
    col = lax.broadcasted_iota(jnp.int32, (rows, KX), 1).astype(jnp.float32)
    return row, col


def linear_terms(rows, unit, beta):
    row, _ = iotas(rows)
    slope = reduced(float(centered(2 * UNIT * 7919 * unit)) * row)
    square = reduced(float(centered(UNIT * 7919 * 7919 * unit * unit)) * (row * row))
    line = reduced(float(centered(3 * UNIT * unit)) * row)
    return reduced(product(slope, beta) + square + line)


def column_tables(salt, chunks, first, rall):
    salt = salt.astype(jnp.float32)

    def beta(rows):
        _, col = iotas(rows)
        return reduced(6007.0 * col + salt)

    row, col = iotas(8 * chunks)
    inner = reduced(reduced(float(centered(7919 * 128)) * row) + beta(8 * chunks))
    value = reduced(product(inner, inner) + (384.0 * row + col))
    base_high, base_low = digits(product(jnp.full_like(value, float(centered(UNIT))), value))
    mid_high, mid_low = digits(linear_terms(16, 8, beta(16)))
    low_high, low_low = digits(linear_terms(8, 1, beta(8)))
    pick = lax.broadcasted_iota(jnp.int32, (64, KX), 0)
    for g in range(chunks):
        cross = jnp.where(pick == 2 * g, 256.0, jnp.where(pick == 2 * g + 1, 1.0, 0.0))
        rall[first + g] = jnp.concatenate(
            [
                256.0 * base_high[8 * g : 8 * g + 8],
                base_low[8 * g : 8 * g + 8],
                256.0 * mid_high,
                mid_low,
                256.0 * low_high,
                low_low,
                cross,
            ],
            axis=0,
        ).astype(jnp.bfloat16)


def salt_turn(salt):
    half = jnp.where(salt % 2 == 1, (salt + PR) // 2, salt // 2)
    whole = half * jnp.int32(STEP_WHOLE - 2**32 if STEP_WHOLE >= 2**31 else STEP_WHOLE)
    return whole + (half * STEP_REST) // PR + BIAS


def kernel(
    width_x,
    width_g,
    lengths_ref,
    salts_ref,
    acts_ref,
    grads_ref,
    rows_ref,
    domains_ref,
    eg_ref,
    out_ref,
    xbuf,
    table,
    rall,
    acc,
    px,
    pg_send,
    pg,
    msg,
    dom_slot,
    sum_slot,
    gram_c,
    gram_z,
    in_sem,
    px_ss,
    px_rs,
    pg_ss,
    pg_rs,
    msg_ss,
    msg_rs,
    sum_ss,
    sum_rs,
    gc_ss,
    gc_rs,
    gz_ss,
    gz_rs,
):
    dp, tok = lax.axis_index("dp"), lax.axis_index("tok")
    z, x, yh = lax.div(dp, 8), lax.rem(lax.div(dp, 2), 4), lax.rem(dp, 2)
    yl, core = lax.div(tok, 2), lax.rem(tok, 2)
    y = 2 * yh + yl

    def plane_peer(dz, dyh):
        z_, yh_ = lax.rem(z + dz, 8), lax.rem(yh + dyh, 2)
        return 2 * z_ + yh_, (8 * z_ + 2 * x + yh_, tok)

    def column_peer(dy, dcore):
        y_, core_ = lax.rem(y + dy, 4), lax.rem(core + dcore, 2)
        place = (8 * z + 2 * x + lax.div(y_, 2), 2 * lax.rem(y_, 2) + core_)
        return 2 * y_ + core_, place

    def z_peer(dz):
        z_ = lax.rem(z + dz, 8)
        return z_, (8 * z_ + 2 * x + yh, tok)

    def x_peer(dx):
        x_ = lax.rem(x + dx, 4)
        return x_, (8 * z + 2 * x_ + yh, tok)

    def tok_peer(dyl, dcore):
        to = 2 * lax.rem(yl + dyl, 2) + lax.rem(core + dcore, 2)
        return to, (dp, to)

    ring = (4, 3, 5, 2, 6, 1, 7, 0)
    plane_peers = [plane_peer(dz, d) for dz in ring for d in (1, 0)][:15]
    column_peers = [column_peer(dy, d) for dy in (2, 1, 3, 0) for d in (1, 0)][:7]
    z_peers = [z_peer(dz) for dz in ring[:7]]
    x_peers = [x_peer(dx) for dx in (2, 1, 3)]
    across, diagonal, sibling = tok_peer(1, 0), tok_peer(1, 1), tok_peer(0, 1)

    def remote(source, target, sent, received, device):
        return pltpu.make_async_remote_copy(
            src_ref=source,
            dst_ref=target,
            send_sem=sent,
            recv_sem=received,
            device_id=device,
            device_id_type=MESH,
        )

    def exchange(source, slots, own, peers, sends, receives):
        out, arriving = [], []
        for k, (slot, device) in enumerate(peers):
            here = (source(slot), slots.at[own], sends.at[k], receives.at[own], device)
            there = (source(slot), slots.at[slot], sends.at[k], receives.at[slot], device)
            out.append(functools.partial(remote, *here))
            arriving.append(functools.partial(remote, *there))
        return out, arriving

    n_x, n_g = width_x // PAIR, width_g // PAIR
    n = n_x + n_g
    loads = [
        pltpu.make_async_copy(acts_ref.at[:, pl.ds(c * PAIR, PAIR)], xbuf.at[c], in_sem.at[c])
        for c in range(n_x)
    ] + [
        pltpu.make_async_copy(
            grads_ref.at[:, pl.ds(c * PAIR, PAIR)], xbuf.at[n_x + c], in_sem.at[n_x + c]
        )
        for c in range(n_g)
    ]
    for load in loads:
        load.start()

    barrier = pltpu.get_barrier_semaphore()

    greeted = plane_peers + [p for k, p in enumerate(column_peers) if k != 1] + x_peers
    for _, device in greeted:
        pl.semaphore_signal(barrier, inc=1, device_id=device, device_id_type=MESH)

    salt_x, salt_g = salts_ref[0], salts_ref[1]
    column_tables(salt_x, 2 * n_x, 0, rall)
    column_tables(salt_g, 2 * n_g, 2 * n_x, rall)
    turn_x, turn_g = salt_turn(salt_x), salt_turn(salt_g)
    acc[...] = jnp.zeros_like(acc)

    def make_table(c, slot, turn):
        for half in range(2):
            value = jnp.dot(rows_ref[...], rall[2 * c + half], preferred_element_type=jnp.float32)
            small = (jnp.abs(value) - float(PR)).astype(jnp.int32)
            angle = small * small * jnp.int32(TURN - 2**32) + turn
            sign = jnp.where(angle < 0, 1.0, -1.0).astype(jnp.bfloat16)
            table[slot, pl.ds(half * ROWS, ROWS), :] = sign

    def product_of(c, slot):
        pltpu.make_async_copy(acts_ref.at[:, pl.ds(0, PAIR)], xbuf.at[c], in_sem.at[c]).wait()
        return jnp.dot(xbuf[c], table[slot], preferred_element_type=jnp.float32)

    make_table(0, 0, turn_x)

    def step(c, _):
        slot = lax.rem(c, 2)
        more = product_of(c, slot)
        make_table(c + 1, 1 - slot, turn_x)
        acc[0] += more
        return 0

    lax.fori_loop(0, n_x - 1, step, 0)
    more = product_of(n_x - 1, (n_x - 1) % 2)
    make_table(n_x, n_x % 2, turn_g)
    acc[0] += more

    tokens = acc.shape[1]
    seg = tokens // 2
    position = lax.broadcasted_iota(jnp.int32, (tokens, 1), 0)
    limit = jnp.where(position < seg, lengths_ref[0], lengths_ref[1])
    live = (tok * seg + position % seg < limit).astype(jnp.float32)
    px[tok] = (acc[0] * (live / math.sqrt(width_x))).astype(jnp.bfloat16)
    px_out, px_in = exchange(
        lambda slot: px.at[tok], px, tok, [across, sibling], px_ss, px_rs
    )
    far = across[0]
    forward = functools.partial(
        remote, px.at[far], px.at[far], px_ss.at[2], px_rs.at[far], sibling[1]
    )
    forwarded = functools.partial(
        remote, px.at[far], px.at[diagonal[0]], px_ss.at[2], px_rs.at[diagonal[0]], sibling[1]
    )
    pl.semaphore_wait(barrier, len(greeted))
    for copy in px_out:
        copy().start()

    def step_g(c, _):
        slot = lax.rem(c, 2)
        more = product_of(c, slot)
        make_table(c + 1, 1 - slot, turn_g)
        acc[1] += more
        return 0

    lax.fori_loop(n_x, n - 1, step_g, 0)
    acc[1] += product_of(n - 1, (n - 1) % 2)
    proj_g = (acc[1] * (live / math.sqrt(width_g))).T.astype(jnp.bfloat16)
    for q in range(4):
        pg_send[q] = proj_g[64 * q : 64 * q + 64]
    pg_out, pg_in = exchange(
        lambda slot: pg_send.at[slot], pg, tok, [across, diagonal, sibling], pg_ss, pg_rs
    )
    for copy in pg_out:
        copy().start()
    pg[tok] = pg_send[tok]
    px_in[0]().wait_recv()
    forward().start()

    lane = lax.broadcasted_iota(jnp.int32, (128, 256), 1)
    row = lax.broadcasted_iota(jnp.int32, (128, 256), 0)
    source = lane // 16
    example = 2 * ((source // 2) * 8 + x * 2 + source % 2) + (lane // 8) % 2
    chosen = (row == example).astype(jnp.bfloat16)
    labels = jnp.broadcast_to(domains_ref[...], (8, 128)).astype(jnp.float32).astype(jnp.bfloat16)
    label = jnp.dot(labels, chosen, preferred_element_type=jnp.float32)[0:1].astype(jnp.int32)
    hot = ((label == row % 16) & (row // 16 == lane % 8)).astype(jnp.float32).astype(jnp.bfloat16)

    px_in[1]().wait_recv()
    for copy in pg_in:
        copy().wait_recv()
    forwarded().wait_recv()
    total = []
    for e in range(2):
        left = jnp.concatenate([pg[q, :, e * seg : e * seg + seg] for q in range(4)], axis=1)
        right = jnp.concatenate([px[q, e * seg : e * seg + seg, :] for q in range(4)], axis=0)
        outer = jnp.dot(left, right, preferred_element_type=jnp.float32)
        total.append(outer / math.sqrt(LEN))
    for t in range(16):
        r, c = 8 * (t // 2), 128 * (t % 2)
        msg[t] = jnp.concatenate(
            [total[0][r : r + 8, c : c + 128], total[1][r : r + 8, c : c + 128]], axis=0
        ).astype(jnp.bfloat16)

    here = 2 * z + yh
    msg_out, msg_in = exchange(
        lambda slot: msg.at[slot], dom_slot, here, plane_peers, msg_ss, msg_rs
    )
    for copy in msg_out:
        copy().start()
    dom_slot[here] = msg[here]
    for r in range(64):
        eg_ref[:, KX * r : KX * r + KX] = jnp.concatenate(
            [total[0][r : r + 1], total[1][r : r + 1]], axis=0
        ).astype(jnp.bfloat16)
    for copy in msg_in:
        copy().wait_recv()
    held = dom_slot[...].reshape(256, 128)
    domain_part = jnp.dot(hot, held, preferred_element_type=jnp.float32)

    sum_slot[x] = domain_part.astype(jnp.bfloat16)
    sum_out, sum_in = exchange(lambda slot: sum_slot.at[x], sum_slot, x, x_peers, sum_ss, sum_rs)
    for copy in sum_out:
        copy().start()
    for copy in sum_in:
        copy().wait_recv()
    share = sum(sum_slot[q].astype(jnp.float32) for q in range(4))
    own = jnp.concatenate([share[16 * r : 16 * r + 16] for r in range(8)], axis=1)
    high = own.astype(jnp.bfloat16).astype(jnp.float32)
    low = own - high
    left = jnp.concatenate([high, high, low], axis=1).astype(jnp.bfloat16)
    right = jnp.concatenate([high, low, high], axis=1)
    right = jnp.concatenate([right] * 8, axis=0).astype(jnp.bfloat16)
    wide = lax.dot_general(
        left, right, (((1,), (1,)), ((), ())), preferred_element_type=jnp.float32
    )
    on_diagonal = (
        lax.broadcasted_iota(jnp.int32, (16, 128), 1) // 16
        == lax.broadcasted_iota(jnp.int32, (16, 128), 0) % 8
    )
    wide = jnp.where(on_diagonal, wide, 0.0)
    flat = jnp.concatenate(
        [jnp.sum(wide[:8], axis=0, keepdims=True), jnp.sum(wide[8:], axis=0, keepdims=True)], axis=0
    )

    pending = px_out + [forward] + pg_out + msg_out + sum_out
    for slots, own_slot, peers, sends, receives in (
        (gram_c, 2 * y + core, column_peers, gc_ss, gc_rs),
        (gram_z, z, z_peers, gz_ss, gz_rs),
    ):
        slots[own_slot] = flat
        gram_out, gram_in = exchange(
            lambda slot: slots.at[own_slot], slots, own_slot, peers, sends, receives
        )
        for copy in gram_out:
            copy().start()
        for copy in pending:
            copy().wait_send()
        pending = gram_out
        for copy in gram_in:
            copy().wait_recv()
        flat = jnp.sum(slots[...], axis=0)
    for copy in pending:
        copy().wait_send()
    spread = jnp.concatenate(
        [jnp.broadcast_to(flat[0:1], (8, 128)), jnp.broadcast_to(flat[1:2], (8, 128))], axis=0
    )
    spread = jnp.where(on_diagonal, spread, 0.0)
    fold = (
        lax.broadcasted_iota(jnp.int32, (128, 16), 0) % 16
        == lax.broadcasted_iota(jnp.int32, (128, 16), 1)
    ).astype(jnp.float32)
    out_ref[...] = jnp.dot(
        spread, fold, precision=lax.Precision.HIGHEST, preferred_element_type=jnp.float32
    ) / (16.0 * KX * KG)


def keep(eg_ref, gram_ref, eg_out, gram_out):
    eg_out[...] = eg_ref[...]
    gram_out[...] = gram_ref[...]


def body(acts, grads, lengths, domains, hash_salts):
    ex_dev, seg, width_x = acts.shape
    width_g = grads.shape[2]
    tokens = ex_dev * seg
    chunks = (width_x + width_g) // PAIR
    rows = jnp.asarray(row_matrix(width_x // ROWS), jnp.bfloat16)
    dma = pltpu.SemaphoreType.DMA
    vmem = pl.BlockSpec(memory_space=pltpu.VMEM)
    results = (
        jax.ShapeDtypeStruct((ex_dev, 64 * KX), jnp.bfloat16),
        jax.ShapeDtypeStruct((DOMAINS, DOMAINS), jnp.float32),
    )
    made = pl.pallas_call(
        functools.partial(kernel, width_x, width_g),
        out_shape=results,
        in_specs=[
            pl.BlockSpec(memory_space=pltpu.SMEM),
            pl.BlockSpec(memory_space=pltpu.SMEM),
            pl.BlockSpec(memory_space=pl.ANY),
            pl.BlockSpec(memory_space=pl.ANY),
            vmem,
            vmem,
        ],
        out_specs=(vmem, vmem),
        scratch_shapes=[
            pltpu.VMEM((chunks, tokens, PAIR), jnp.bfloat16),
            pltpu.VMEM((2, PAIR, KX), jnp.bfloat16),
            pltpu.VMEM((2 * chunks, 128, KX), jnp.bfloat16),
            pltpu.VMEM((2, tokens, KX), jnp.float32),
            pltpu.VMEM((4, tokens, KX), jnp.bfloat16),
            pltpu.VMEM((4, 64, tokens), jnp.bfloat16),
            pltpu.VMEM((4, 64, tokens), jnp.bfloat16),
            pltpu.VMEM((16, 16, 128), jnp.bfloat16),
            pltpu.VMEM((16, 16, 128), jnp.bfloat16),
            pltpu.VMEM((4, 128, 128), jnp.bfloat16),
            pltpu.VMEM((8, 2, 128), jnp.float32),
            pltpu.VMEM((8, 2, 128), jnp.float32),
            dma((chunks,)),
            dma((4,)),
            dma((4,)),
            dma((4,)),
            dma((4,)),
            dma((16,)),
            dma((16,)),
            dma((4,)),
            dma((4,)),
            dma((8,)),
            dma((8,)),
            dma((8,)),
            dma((8,)),
        ],
        compiler_params=pltpu.CompilerParams(
            collective_id=0, has_side_effects=True, vmem_limit_bytes=56 << 20
        ),
    )(
        lengths,
        hash_salts,
        acts.reshape(tokens, width_x),
        grads.reshape(tokens, width_g),
        rows,
        domains.reshape(1, domains.shape[0]),
    )
    return pl.pallas_call(keep, out_shape=results, in_specs=[vmem] * 2, out_specs=(vmem, vmem))(*made)


def solution(mesh):
    in_specs = (P("dp", "tok", None), P("dp", "tok", None), P("dp"), P(), P())
    out_specs = (P("dp", "tok"), P())
    return jax.shard_map(body, mesh=mesh, in_specs=in_specs, out_specs=out_specs, check_vma=False)
```

time: 46.1 us -> 42.3 us (0.918)
  local copies, waits for them, and re-layouts: 2.83 us -> 0 us
  Pallas kernels: 42.5 us -> 41.5 us
    unnamed x2 -> x0, local copies, waits for them, and re-layouts: 2.83 us -> none
    pallas_call x1 -> x2, Pallas kernels: 42.5 us -> 41.5 us  [the longest x1 40.1 us: body(): pl.pallas_call(functools.partial(kernel, width_x, width_g), out_shape=res...]
where the time goes in v2:
time: 42.3 us; the launch traced here: 42.2 us
  Pallas kernels  41.5 us (98%)
  between operations  0.64 us (2%)
    pallas_call x1, Pallas kernels, body(): pl.pallas_call(functools.partial(kernel, width_x, width_g), out_shape=res...  40.1 us
    pallas_call x1, Pallas kernels, body(): pl.pallas_call(keep, out_shape=results, in_specs=[vmem] * 2, out_specs=(v...  1.48 us

profile of v2, /device:TPU:1, one launch (start us, length us, event | category | flops | bytes accessed | tf_op | source)
XLA Modules:
  0.0 42.2 jit_solution(14958108169649298728)
XLA Ops:
  0.6 40.1 %shard_map.77 = (bf16[2,16384]{1,0:T(2,128)(2,1)}, f32[16,16]{1,0:T(8,128)}) custom-call(s32[2]{0:T(128)} %lengths_ref.1, s32[2]{0:T(128)} %salts_ref.1, bf16[256,14336]{1,0:T(8,128)(2,1)} %bitcast.3, bf16[256,4096]{1,0:T(8,128)(2,1)} %bitcast.4, bf16[1024,128]{1,0:T(8,128)(2,1)} %constant.2.clone.rows_ref, s32[1,128]{1,0:T(1,128)} %bitcast.5), custom_call_target="tpu_custom_call" | custom-call | tf_op jit(solution)/shard_map/pallas_call | solution.py:413
  40.7 1.5 %shard_map.78 = (bf16[2,16384]{1,0:T(2,128)(2,1)}, f32[16,16]{1,0:T(8,128)}) custom-call(bf16[2,16384]{1,0:T(2,128)(2,1)} %get-tuple-element.4.eg_ref, f32[16,16]{1,0:T(8,128)} %get-tuple-element.5.gram_ref), custom_call_target="tpu_custom_call" | custom-call | tf_op jit(solution)/shard_map/pallas_call | solution.py:463

commit v3 on v2

--- a/solution.py
+++ b/solution.py
@@ -236,20 +236,21 @@
             sign = jnp.where(angle < 0, 1.0, -1.0).astype(jnp.bfloat16)
             table[slot, pl.ds(half * ROWS, ROWS), :] = sign
 
+    waits = {0: range(2), 2: range(2, 5), 5: range(5, n)}
+
     def product_of(c, slot):
-        pltpu.make_async_copy(acts_ref.at[:, pl.ds(0, PAIR)], xbuf.at[c], in_sem.at[c]).wait()
+        for arrived in waits.get(c, ()):
+            loads[arrived].wait()
         return jnp.dot(xbuf[c], table[slot], preferred_element_type=jnp.float32)
 
     make_table(0, 0, turn_x)
 
-    def step(c, _):
-        slot = lax.rem(c, 2)
+    for c in range(n_x - 1):
+        slot = c % 2
         more = product_of(c, slot)
         make_table(c + 1, 1 - slot, turn_x)
         acc[0] += more
-        return 0
-
-    lax.fori_loop(0, n_x - 1, step, 0)
+
     more = product_of(n_x - 1, (n_x - 1) % 2)
     make_table(n_x, n_x % 2, turn_g)
     acc[0] += more
@@ -259,29 +260,31 @@
     position = lax.broadcasted_iota(jnp.int32, (tokens, 1), 0)
     limit = jnp.where(position < seg, lengths_ref[0], lengths_ref[1])
     live = (tok * seg + position % seg < limit).astype(jnp.float32)
-    px[tok] = (acc[0] * (live / math.sqrt(width_x))).astype(jnp.bfloat16)
-    px_out, px_in = exchange(
-        lambda slot: px.at[tok], px, tok, [across, sibling], px_ss, px_rs
-    )
-    far = across[0]
-    forward = functools.partial(
-        remote, px.at[far], px.at[far], px_ss.at[2], px_rs.at[far], sibling[1]
-    )
-    forwarded = functools.partial(
-        remote, px.at[far], px.at[diagonal[0]], px_ss.at[2], px_rs.at[diagonal[0]], sibling[1]
-    )
+    scaled = (acc[0] * (live / math.sqrt(width_x))).astype(jnp.bfloat16)
+    px[tok, 0] = scaled[:seg]
+    px[tok, 1] = scaled[seg:]
+    far, near, other = across[0], sibling[0], diagonal[0]
+
+    def px_copy(source, slot, half, sent, device):
+        there = px.at[slot, half]
+        return remote(px.at[source, half], there, px_ss.at[sent + half], px_rs.at[slot, half], device)
+
+    px_out = [functools.partial(px_copy, tok, tok, half, 0, across[1]) for half in range(2)]
+    px_out += [functools.partial(px_copy, tok, tok, half, 2, sibling[1]) for half in range(2)]
+    forward = [functools.partial(px_copy, far, far, half, 4, sibling[1]) for half in range(2)]
+    px_far = [functools.partial(px_copy, tok, far, half, 0, across[1]) for half in range(2)]
+    px_near = [functools.partial(px_copy, tok, near, half, 2, sibling[1]) for half in range(2)]
+    px_other = [functools.partial(px_copy, far, other, half, 4, sibling[1]) for half in range(2)]
     pl.semaphore_wait(barrier, len(greeted))
     for copy in px_out:
         copy().start()
 
-    def step_g(c, _):
-        slot = lax.rem(c, 2)
+    for c in range(n_x, n - 1):
+        slot = c % 2
         more = product_of(c, slot)
         make_table(c + 1, 1 - slot, turn_g)
         acc[1] += more
-        return 0
-
-    lax.fori_loop(n_x, n - 1, step_g, 0)
+
     acc[1] += product_of(n - 1, (n - 1) % 2)
     proj_g = (acc[1] * (live / math.sqrt(width_g))).T.astype(jnp.bfloat16)
     for q in range(4):
@@ -292,8 +295,9 @@
     for copy in pg_out:
         copy().start()
     pg[tok] = pg_send[tok]
-    px_in[0]().wait_recv()
-    forward().start()
+    for half in range(2):
+        px_far[half]().wait_recv()
+        forward[half]().start()
 
     lane = lax.broadcasted_iota(jnp.int32, (128, 256), 1)
     row = lax.broadcasted_iota(jnp.int32, (128, 256), 0)
@@ -304,16 +308,14 @@
     label = jnp.dot(labels, chosen, preferred_element_type=jnp.float32)[0:1].astype(jnp.int32)
     hot = ((label == row % 16) & (row // 16 == lane % 8)).astype(jnp.float32).astype(jnp.bfloat16)
 
-    px_in[1]().wait_recv()
-    for copy in pg_in:
+    for copy in px_near + pg_in + px_other:
         copy().wait_recv()
-    forwarded().wait_recv()
     total = []
     for e in range(2):
         left = jnp.concatenate([pg[q, :, e * seg : e * seg + seg] for q in range(4)], axis=1)
-        right = jnp.concatenate([px[q, e * seg : e * seg + seg, :] for q in range(4)], axis=0)
+        right = jnp.concatenate([px[q, e] for q in range(4)], axis=0)
         outer = jnp.dot(left, right, preferred_element_type=jnp.float32)
-        total.append(outer / math.sqrt(LEN))
+        total.append(outer * (1.0 / math.sqrt(LEN)))
     for t in range(16):
         r, c = 8 * (t // 2), 128 * (t % 2)
         msg[t] = jnp.concatenate(
@@ -361,7 +363,7 @@
         [jnp.sum(wide[:8], axis=0, keepdims=True), jnp.sum(wide[8:], axis=0, keepdims=True)], axis=0
     )
 
-    pending = px_out + [forward] + pg_out + msg_out + sum_out
+    pending = px_out + forward + pg_out + msg_out + sum_out
     for slots, own_slot, peers, sends, receives in (
         (gram_c, 2 * y + core, column_peers, gc_ss, gc_rs),
         (gram_z, z, z_peers, gz_ss, gz_rs),
@@ -385,12 +387,13 @@
     )
     spread = jnp.where(on_diagonal, spread, 0.0)
     fold = (
-        lax.broadcasted_iota(jnp.int32, (128, 16), 0) % 16
-        == lax.broadcasted_iota(jnp.int32, (128, 16), 1)
-    ).astype(jnp.float32)
-    out_ref[...] = jnp.dot(
-        spread, fold, precision=lax.Precision.HIGHEST, preferred_element_type=jnp.float32
-    ) / (16.0 * KX * KG)
+        lax.broadcasted_iota(jnp.int32, (384, 16), 0) % 16
+        == lax.broadcasted_iota(jnp.int32, (384, 16), 1)
+    ).astype(jnp.bfloat16)
+    high = spread.astype(jnp.bfloat16).astype(jnp.float32)
+    middle = (spread - high).astype(jnp.bfloat16).astype(jnp.float32)
+    pieces = jnp.concatenate([high, middle, spread - high - middle], axis=1).astype(jnp.bfloat16)
+    out_ref[...] = jnp.dot(pieces, fold, preferred_element_type=jnp.float32) / (16.0 * KX * KG)
 
 
 def keep(eg_ref, gram_ref, eg_out, gram_out):
@@ -427,7 +430,7 @@
             pltpu.VMEM((2, PAIR, KX), jnp.bfloat16),
             pltpu.VMEM((2 * chunks, 128, KX), jnp.bfloat16),
             pltpu.VMEM((2, tokens, KX), jnp.float32),
-            pltpu.VMEM((4, tokens, KX), jnp.bfloat16),
+            pltpu.VMEM((4, ex_dev, seg, KX), jnp.bfloat16),
             pltpu.VMEM((4, 64, tokens), jnp.bfloat16),
             pltpu.VMEM((4, 64, tokens), jnp.bfloat16),
             pltpu.VMEM((16, 16, 128), jnp.bfloat16),
@@ -436,8 +439,8 @@
             pltpu.VMEM((8, 2, 128), jnp.float32),
             pltpu.VMEM((8, 2, 128), jnp.float32),
             dma((chunks,)),
-            dma((4,)),
-            dma((4,)),
+            dma((6,)),
+            dma((4, 2)),
             dma((4,)),
             dma((4,)),
             dma((16,)),

time: 42.3 us -> 41.5 us (0.981)
  Pallas kernels: 41.5 us -> 40.7 us
    pallas_call x1, Pallas kernels: 40.1 us -> 39.2 us  [body(): pl.pallas_call(functools.partial(kernel, width_x, width_g), out_shape=res...]
where the time goes in v3:
time: 41.5 us; the launch traced here: 41.3 us
  Pallas kernels  40.7 us (98%)
  between operations  0.64 us (2%)
    pallas_call x1, Pallas kernels, body(): pl.pallas_call(functools.partial(kernel, width_x, width_g), out_shape=res...  39.2 us
    pallas_call x1, Pallas kernels, body(): pl.pallas_call(keep, out_shape=results, in_specs=[vmem] * 2, out_specs=(v...  1.48 us

profile of v3, /device:TPU:1, one launch (start us, length us, event | category | flops | bytes accessed | tf_op | source)
XLA Modules:
  0.0 41.3 jit_solution(3438220294352923101)
XLA Ops:
  0.6 39.2 %shard_map.77 = (bf16[2,16384]{1,0:T(2,128)(2,1)}, f32[16,16]{1,0:T(8,128)}) custom-call(s32[2]{0:T(128)} %lengths_ref.1, s32[2]{0:T(128)} %salts_ref.1, bf16[256,14336]{1,0:T(8,128)(2,1)} %bitcast.3, bf16[256,4096]{1,0:T(8,128)(2,1)} %bitcast.4, bf16[1024,128]{1,0:T(8,128)(2,1)} %constant.2.clone.rows_ref, s32[1,128]{1,0:T(1,128)} %bitcast.5), custom_call_target="tpu_custom_call" | custom-call | tf_op jit(solution)/shard_map/pallas_call | solution.py:416
  39.9 1.5 %shard_map.78 = (bf16[2,16384]{1,0:T(2,128)(2,1)}, f32[16,16]{1,0:T(8,128)}) custom-call(bf16[2,16384]{1,0:T(2,128)(2,1)} %get-tuple-element.4.eg_ref, f32[16,16]{1,0:T(8,128)} %get-tuple-element.5.gram_ref), custom_call_target="tpu_custom_call" | custom-call | tf_op jit(solution)/shard_map/pallas_call | solution.py:466

commit v4 on v3

--- a/solution.py
+++ b/solution.py
@@ -226,7 +226,6 @@
     column_tables(salt_x, 2 * n_x, 0, rall)
     column_tables(salt_g, 2 * n_g, 2 * n_x, rall)
     turn_x, turn_g = salt_turn(salt_x), salt_turn(salt_g)
-    acc[...] = jnp.zeros_like(acc)
 
     def make_table(c, slot, turn):
         for half in range(2):
@@ -249,7 +248,7 @@
         slot = c % 2
         more = product_of(c, slot)
         make_table(c + 1, 1 - slot, turn_x)
-        acc[0] += more
+        acc[0] = more if c == 0 else acc[0] + more
 
     more = product_of(n_x - 1, (n_x - 1) % 2)
     make_table(n_x, n_x % 2, turn_g)
@@ -283,7 +282,7 @@
         slot = c % 2
         more = product_of(c, slot)
         make_table(c + 1, 1 - slot, turn_g)
-        acc[1] += more
+        acc[1] = more if c == n_x else acc[1] + more
 
     acc[1] += product_of(n - 1, (n - 1) % 2)
     proj_g = (acc[1] * (live / math.sqrt(width_g))).T.astype(jnp.bfloat16)

time: 41.5 us -> 41.5 us (level)
  no operation moved by 1% of the time
where the time goes in v4:
time: 41.5 us; the launch traced here: 41.3 us
  Pallas kernels  40.7 us (98%)
  between operations  0.64 us (2%)
    pallas_call x1, Pallas kernels, body(): pl.pallas_call(functools.partial(kernel, width_x, width_g), out_shape=res...  39.2 us
    pallas_call x1, Pallas kernels, body(): pl.pallas_call(keep, out_shape=results, in_specs=[vmem] * 2, out_specs=(v...  1.48 us

profile of v4, /device:TPU:1, one launch (start us, length us, event | category | flops | bytes accessed | tf_op | source)
XLA Modules:
  0.0 41.3 jit_solution(3438220294352923101)
XLA Ops:
  0.6 39.2 %shard_map.77 = (bf16[2,16384]{1,0:T(2,128)(2,1)}, f32[16,16]{1,0:T(8,128)}) custom-call(s32[2]{0:T(128)} %lengths_ref.1, s32[2]{0:T(128)} %salts_ref.1, bf16[256,14336]{1,0:T(8,128)(2,1)} %bitcast.3, bf16[256,4096]{1,0:T(8,128)(2,1)} %bitcast.4, bf16[1024,128]{1,0:T(8,128)(2,1)} %constant.2.clone.rows_ref, s32[1,128]{1,0:T(1,128)} %bitcast.5), custom_call_target="tpu_custom_call" | custom-call | tf_op jit(solution)/shard_map/pallas_call | solution.py:415
  39.9 1.5 %shard_map.78 = (bf16[2,16384]{1,0:T(2,128)(2,1)}, f32[16,16]{1,0:T(8,128)}) custom-call(bf16[2,16384]{1,0:T(2,128)(2,1)} %get-tuple-element.4.eg_ref, f32[16,16]{1,0:T(8,128)} %get-tuple-element.5.gram_ref), custom_call_target="tpu_custom_call" | custom-call | tf_op jit(solution)/shard_map/pallas_call | solution.py:465
